TPU v7x, 32 devices: a whole 2x2x4 slice. The times are simulated.
32 devices in a mesh: grp: 2 (over y), run: 4 (over x, core), chan: 4 (over z).
Axes of the slice: x: 2, y: 2, z: 4, core: 2. Of those that a mesh axis runs over, the one named last changes fastest.
Arguments:
- embed: bfloat16 [512, 8192], P('grp', 'chan'), parts along dimension 0, may hold values from -6 to 6
- noise: bfloat16 [16, 32, 8192], P(('grp', 'run'), None, 'chan'), parts along dimension 0, may hold values from -12 to 12
- positions: int32 [16, 32], P(('grp', 'run')), parts along dimension 0, may hold values from 0 to 255
- restore: int32 [16, 2], P(('grp', 'run')), parts along dimension 0, may hold values 0 or 1
- short_one: float32 [7, 8192], P(None, 'chan'), may hold values from -2 to 2
- long_one: float32 [128, 8192], P(None, 'chan'), may hold values from -0.5 to 0.5
- out_weight: bfloat16 [8192, 8192], P(None, 'chan'), may hold values from -0.0625 to 0.0625
- short_two: float32 [7, 8192], P(None, 'chan'), may hold values from -2 to 2
- long_two: float32 [128, 8192], P(None, 'chan'), may hold values from -0.5 to 0.5
Outputs:
- traced: bfloat16 [16, 256, 8192], P(('grp', 'run'), None, 'chan'), parts along dimension 0
There are 2 independent parts, one for each index of `grp`. A program takes and returns all parts, laid end to end along the dimension named above; an argument that names none is the same for every part. Nothing has to cross between parts.
All inputs are finite; a program needn't handle non-finite values. No bound on the sum of `restore` on one device may be relied on, other than what follows from the above.
Results may differ from a plain program's by a relative error of at most 0.007.
Values may be sent and summed in bfloat16 or wider, within the bound.
A program may use at most 128 MiB of HBM per device.

v0:
```python
import jax
import jax.numpy as jnp
from jax import lax
from jax.sharding import PartitionSpec as P


def short_filter(field, filter_taps):
    length = field.shape[1]
    running = jnp.zeros(field.shape, jnp.float32)
    for shift_count in range(filter_taps.shape[0]):
        shifted = jnp.pad(field, ((0, 0), (shift_count, 0), (0, 0)))[:, :length]
        running = running + filter_taps[shift_count][None, None, :] * shifted
    return running


def block_filter(field, filter_taps):
    width = field.shape[2]
    span = filter_taps.shape[0]
    kernel = filter_taps[::-1][:, None, :]
    return lax.conv_general_dilated(
        field,
        kernel,
        window_strides=(1,),
        padding=((span - 1, 0),),
        dimension_numbers=("NWC", "WIO", "NWC"),
        feature_group_count=width,
        precision=lax.Precision.HIGHEST,
        preferred_element_type=jnp.float32,
    )


def per_device(
    embed, noise, positions, restore, short_one, long_one, out_weight, short_two, long_two
):
    run_count = noise.shape[0]
    length = embed.shape[0]
    first_run = lax.axis_index("run") * run_count
    run_ids = first_run + jnp.arange(run_count, dtype=jnp.int32)
    onehot = (jnp.arange(length, dtype=jnp.int32)[None, :, None] == positions[:, None, :]).astype(
        jnp.bfloat16
    )
    added = jnp.einsum("rlp,rpc->rlc", onehot, noise, preferred_element_type=jnp.float32)
    corrupt_flag = (run_ids != 0).astype(jnp.float32)[:, None, None]
    inputs = (embed.astype(jnp.float32)[None] + corrupt_flag * added).astype(jnp.bfloat16)
    batch_inputs = jnp.concatenate([inputs, embed[None]], axis=0)
    input_values = batch_inputs.astype(jnp.float32)
    filtered = block_filter(short_filter(input_values, short_one), long_one)
    mixed = (filtered * jax.nn.silu(input_values)).astype(jnp.bfloat16)
    initial = jnp.zeros((mixed.shape[0], length, out_weight.shape[1]), jnp.float32)
    segment = lax.all_gather(mixed, "chan", axis=2, tiled=True)
    weight_rows = lax.slice_in_dim(out_weight, 0, segment.shape[2], axis=0)
    projected = initial + jnp.einsum(
        "rlk,kc->rlc", segment, weight_rows, preferred_element_type=jnp.float32
    )
    hidden = (input_values + projected).astype(jnp.bfloat16)
    clean_hidden = hidden[run_count]
    hidden = hidden[:run_count]
    block_size = length // restore.shape[1]
    restored_rows = jnp.repeat(restore, block_size, axis=1)[:, :, None] == 1
    restored = jnp.where(restored_rows, clean_hidden[None], hidden)
    restored_values = restored.astype(jnp.float32)
    second = block_filter(short_filter(restored_values, short_two), long_two)
    return (restored_values + second * jax.nn.silu(restored_values)).astype(jnp.bfloat16)


def solution(mesh):
    in_specs = (
        P("grp", "chan"),
        P(("grp", "run"), None, "chan"),
        P(("grp", "run"), None),
        P(("grp", "run"), None),
        P(None, "chan"),
        P(None, "chan"),
        P(None, "chan"),
        P(None, "chan"),
        P(None, "chan"),
    )
    out_specs = P(("grp", "run"), None, "chan")
    return jax.shard_map(
        per_device, mesh=mesh, in_specs=in_specs, out_specs=out_specs, check_vma=False
    )
```

profile of v0, /device:TPU:0, one launch (start us, length us, event | category | flops | bytes accessed | tf_op | source)
XLA Modules:
  0.0 446.8 jit_solution(15623138889471099007)
XLA Ops:
  6.5 0.0 copy-start
  6.5 0.0 copy-start.6
  6.5 0.0 all-gather.2.cloned.1.call-start
  6.5 1.2 fusion.40
  7.8 0.0 copy-start.2
  7.8 2.9 convert_element_type.53
  10.7 8.9 %rev.6 = f32[128,2048]{1,0:T(8,128)} reverse(f32[128,2048]{1,0:T(8,128)} %param.14), dimensions={0} | reverse | bytes 2097152 | tf_op jit(solution)/shard_map/rev | solution.py:19
  19.5 0.0 copy-done
  19.5 0.0 copy-done.6
  19.5 2.4 add_convert_fusion.1
  22.0 0.0 copy-done.2
  22.0 0.4 maximum_convert_fusion
  22.4 0.0 copy-start.4
  22.4 5.2 %fusion.10 = f32[3,256,2048]{2,1,0:T(8,128)S(1)} fusion(f32[3,256,2048]{2,1,0:T(8,128)S(1)} %maximum_convert_fusion, f32[2048]{0:T(1024)S(1)} %bitcast.48, f32[2048]{0:T(1024)S(1)} %bitcast.49, f32[2048]{0:T(1024)S(1)} %bitcast.44, f32[2048]{0:T(1024)S(1)} %bitcast.45, f32[2048]{0:T(1024)S(1)} %bitcast.46, f32[2048]{0:T(1024)S(1)} %bitcast.47, ...), kind=kLoop, calls=%fused_computation.16 | loop fusion | flops 20447232 | bytes 12640256 | tf_op jit(solution)/shard_map/add | solution.py:12
  27.6 0.0 copy-done.4
  27.6 98.9 %fusion.2 = f32[3,256,2048]{2,0,1:T(4,128)S(1)} fusion(f32[3,256,2048]{2,1,0:T(8,128)S(1)} %fusion.10, f32[128,1,2048]{2,0,1:T(8,128)S(1)} %bitcast.35), kind=kOutput, calls=%fused_computation.2 | convolution fusion | flops 1816657920 | bytes 13631488 | tf_op jit(solution)/shard_map/conv_general_dilated | solution.py:20
  126.5 0.0 copy-start.7
  126.5 5.2 %fusion.16 = bf16[3,256,2048]{2,1,0:T(8,128)(2,1)} fusion(f32[3,256,2048]{2,0,1:T(4,128)S(1)} %fusion.2, bf16[1,256,2048]{2,1,0:T(8,128)(2,1)S(1)} %bitcast.32, bf16[2,256,2048]{2,1,0:T(8,128)(2,1)S(1)} %add_convert_fusion.1), kind=kLoop, calls=%fused_computation.23 | loop fusion | flops 12582912 | bytes 12582912 | tf_op jit(solution)/shard_map/convert_element_type | solution.py:48
  131.7 0.0 copy-start.5
  131.7 0.0 all-gather.2.cloned.1.call-update
  131.8 0.0 copy-done.7
  131.8 0.1 broadcast_bitcast_fusion
  131.9 8.9 %rev.7 = f32[128,2048]{1,0:T(8,128)} reverse(f32[128,2048]{1,0:T(8,128)} %param.17), dimensions={0} | reverse | bytes 2097152 | tf_op jit(solution)/shard_map/rev | solution.py:19
  140.7 0.0 copy-done.5
  140.8 212.0 %all-gather.2.cloned.1.call-done = bf16[3,256,8192]{2,1,0:T(8,128)(2,1)} async-done(((bf16[3,256,2048]{2,1,0:T(8,128)(2,1)}), bf16[3,256,8192]{2,1,0:T(8,128)(2,1)}) %all-gather.2.cloned.1.call-update) | async-done | bytes 12582928 | tf_op jit(solution)/shard_map/all_gather | solution.py:50
  352.8 33.6 %add_convert_fusion = bf16[3,256,2048]{2,1,0:T(8,128)(2,1)S(1)} fusion(bf16[3,256,8192]{2,1,0:T(8,128)(2,1)} %all-gather.2.cloned.1.call-done, bf16[8192,2048]{1,0:T(8,128)(2,1)} %param.15, bf16[1,256,2048]{2,1,0:T(8,128)(2,1)S(1)} %bitcast.33, bf16[2,256,2048]{2,1,0:T(8,128)(2,1)S(1)} %add_convert_fusion.1), kind=kOutput, calls=%fused_computation.24 | convolution fusion | flops 25776095232 | bytes 52428800 | tf_op jit(solution)/shard_map/rlk,kc->rlc/dot_general | solution.py:52
  386.5 0.1 slice_bitcast_fusion
  386.6 0.4 fusion.35
  386.9 0.0 copy-start.3
  386.9 3.5 fusion.23
  390.4 0.0 copy-done.3
  390.4 0.0 copy-start.1
  390.4 45.4 %fusion.31 = f32[2,256,2048]{2,0,1:T(2,128)S(1)} fusion(f32[2,256,2048]{2,1,0:T(8,128)S(1)} %fusion.23, f32[128,1,2048]{2,0,1:T(8,128)S(1)} %bitcast.34), kind=kOutput, calls=%fused_computation.46 | convolution fusion | flops 1211105280 | bytes 9437184 | tf_op jit(solution)/shard_map/conv_general_dilated | solution.py:20
  435.9 4.1 fusion.30
  439.9 0.0 copy-done.1
  (4 shorter events, 0.1 us)
Async XLA Ops:
  6.5 13.0 %copy-start = (bf16[2,32,2048]{2,1,0:T(8,128)(2,1)S(1)}, bf16[2,32,2048]{2,1,0:T(8,128)(2,1)}, u32[]{:S(2)}) copy-start(bf16[2,32,2048]{2,1,0:T(8,128)(2,1)} %param.10) | copy-start | bytes 786436
  6.5 13.0 %copy-start.6 = (s32[2,32]{1,0:T(2,128)S(1)}, s32[2,32]{1,0:T(2,128)}, u32[]{:S(2)}) copy-start(s32[2,32]{1,0:T(2,128)} %param.11) | copy-start | bytes 772
  6.5 346.3 %all-gather.2.cloned.1.call-start = ((), (), s32[]{:S(2)}) async-start(), calls=%async_computation | async-start | bytes 15728640 | tf_op jit(solution)/shard_map/all_gather | solution.py:50
  7.8 14.2 %copy-start.2 = (bf16[256,2048]{1,0:T(8,128)(2,1)S(1)}, bf16[256,2048]{1,0:T(8,128)(2,1)}, u32[]{:S(2)}) copy-start(bf16[256,2048]{1,0:T(8,128)(2,1)} %param.9) | copy-start | bytes 3145732
  22.4 5.2 %copy-start.4 = (f32[128,2048]{1,0:T(8,128)S(1)}, f32[128,2048]{1,0:T(8,128)}, u32[]{:S(2)}) copy-start(f32[128,2048]{1,0:T(8,128)} %rev.6) | copy-start | bytes 3145732
  126.5 5.3 %copy-start.7 = (s32[2,2]{1,0:T(2,128)S(1)}, s32[2,2]{1,0:T(2,128)}, u32[]{:S(2)}) copy-start(s32[2,2]{1,0:T(2,128)} %param.12) | copy-start | bytes 52
  131.7 9.0 %copy-start.5 = (f32[7,2048]{1,0:T(8,128)S(1)}, f32[7,2048]{1,0:T(8,128)}, u32[]{:S(2)}) copy-start(f32[7,2048]{1,0:T(8,128)} %param.16) | copy-start | bytes 172036
  386.9 3.5 copy-start.3
  390.4 49.5 %copy-start.1 = (bf16[2,32,2048]{2,1,0:T(8,128)(2,1)S(1)}, bf16[2,32,2048]{2,1,0:T(8,128)(2,1)}, u32[]{:S(2)}) copy-start(bf16[2,32,2048]{2,1,0:T(8,128)(2,1)} %param.10) | copy-start | bytes 786436
Sparse Core Ops, SparseCore 0:
  131.9 220.8 all-gather.1
where the time goes:
time: 448 us; the launch traced here: 447 us
  waiting for transfers between devices  212 us (47%)
  matrix products  180 us (40%)
  other arithmetic  21.6 us (5%)
  local copies, waits for them, and re-layouts  19.2 us (4%)
  between operations  13.6 us (3%)
    all_gather x1, waiting for transfers between devices, per_device(): segment = lax.all_gather(mixed, 'chan', axis=2, tiled=True)  212 us
    conv_general_dilated x2, matrix products, block_filter(): lax.conv_general_dilated(field, kernel, window_strides=(1,), padding=((sp...  144 us
    dot_general x1, matrix products, per_device(): jnp.einsum('rlk,kc->rlc', segment, weight_rows, preferred_element_type=jn...  33.6 us
    rev x2, local copies, waits for them, and re-layouts, block_filter(): kernel = filter_taps[::-1][:, None, :]  17.7 us
  transfers between devices with their start and end apart: 1, of which 1 were waited for; matrix products, arithmetic and copies ran while one was open for 2% of the time, Pallas kernels for 0%

commit v1 on v0

--- a/solution.py
+++ b/solution.py
@@ -47,7 +47,14 @@
     filtered = block_filter(short_filter(input_values, short_one), long_one)
     mixed = (filtered * jax.nn.silu(input_values)).astype(jnp.bfloat16)
     initial = jnp.zeros((mixed.shape[0], length, out_weight.shape[1]), jnp.float32)
-    segment = lax.all_gather(mixed, "chan", axis=2, tiled=True)
+    ways, here = (lax.axis_size("chan"), lax.axis_index("chan"))
+    segment, reach = (mixed, 1)
+    while reach < ways:
+        theirs = lax.ppermute(segment, "chan", [(d, d ^ reach) for d in range(ways)])
+        mine_first = jnp.concatenate([segment, theirs], axis=2)
+        theirs_first = jnp.concatenate([theirs, segment], axis=2)
+        segment = jnp.where(here & reach == 0, mine_first, theirs_first)
+        reach = 2 * reach
     weight_rows = lax.slice_in_dim(out_weight, 0, segment.shape[2], axis=0)
     projected = initial + jnp.einsum(
         "rlk,kc->rlc", segment, weight_rows, preferred_element_type=jnp.float32

time: 448 us -> 578 us (1.29)
  waiting for transfers between devices: 212 us -> 329 us
  between operations: 13.6 us -> 0.15 us
  other arithmetic: 21.6 us -> 33.4 us
  matrix products: 180 us -> 188 us
    ppermute x0 -> x2, waiting for transfers between devices: none -> 329 us  [per_device(): lax.ppermute(segment, 'chan', [(d, d ^ reach) for d in range(ways)])]
    all_gather x1 -> x0, waiting for transfers between devices: 212 us -> none  [per_device(): segment = lax.all_gather(mixed, 'chan', axis=2, tiled=True)]
    select_n x0 -> x1, other arithmetic: none -> 10.1 us  [per_device(): segment = jnp.where(here & reach == 0, mine_first, theirs_first)]
    dot_general x1, matrix products: 33.6 us -> 41.1 us  [per_device(): jnp.einsum('rlk,kc->rlc', segment, weight_rows, preferred_element_type=jn...]
    ppermute x0 -> x2, starting transfers between devices: none -> 5.78 us  [per_device(): lax.ppermute(segment, 'chan', [(d, d ^ reach) for d in range(ways)])]
  transfers between devices with their start and end apart: 1 -> 2, of which waited for: 1 -> 2; matrix products, arithmetic and copies ran while one was open for 2% -> 2% of each run, Pallas kernels for 0% -> 0%
where the time goes in v1:
time: 578 us; the launch traced here: 577 us
  waiting for transfers between devices  329 us (57%)
  matrix products  188 us (33%)
  other arithmetic  33.4 us (6%)
  local copies, waits for them, and re-layouts  20.4 us (4%)
  starting transfers between devices  5.78 us (1%)
    ppermute x2, waiting for transfers between devices, per_device(): lax.ppermute(segment, 'chan', [(d, d ^ reach) for d in range(ways)])  329 us
    conv_general_dilated x2, matrix products, block_filter(): lax.conv_general_dilated(field, kernel, window_strides=(1,), padding=((sp...  144 us
    dot_general x1, matrix products, per_device(): jnp.einsum('rlk,kc->rlc', segment, weight_rows, preferred_element_type=jn...  41.1 us
    rev x2, local copies, waits for them, and re-layouts, block_filter(): kernel = filter_taps[::-1][:, None, :]  17.7 us
  transfers between devices with their start and end apart: 2, of which 2 were waited for; matrix products, arithmetic and copies ran while one was open for 2% of the time, Pallas kernels for 0%

profile of v1, /device:TPU:0, one launch (start us, length us, event | category | flops | bytes accessed | tf_op | source)
XLA Modules:
  0.0 576.9 jit_solution(16836836126016092585)
XLA Ops:
  0.0 0.0 copy-start
  0.0 0.0 copy-start.2
  0.0 1.2 fusion.47
  1.2 2.8 convert_element_type.53
  4.0 8.9 %rev.6 = f32[128,2048]{1,0:T(8,128)} reverse(f32[128,2048]{1,0:T(8,128)} %param.14), dimensions={0} | reverse | bytes 2097152 | tf_op jit(solution)/shard_map/rev | solution.py:19
  12.9 0.0 copy-done
  12.9 2.4 add_convert_fusion.1
  15.4 0.0 copy-done.2
  15.4 0.4 maximum_convert_fusion
  15.8 0.0 copy-start.5
  15.8 5.2 fusion.16
  21.0 0.0 copy-done.5
  21.0 98.9 %fusion.8 = f32[3,256,2048]{2,0,1:T(4,128)S(1)} fusion(f32[3,256,2048]{2,1,0:T(8,128)S(1)} %fusion.16, f32[128,1,2048]{2,0,1:T(8,128)S(1)} %bitcast.34), kind=kOutput, calls=%fused_computation.9 | convolution fusion | flops 1816657920 | bytes 13631488 | tf_op jit(solution)/shard_map/conv_general_dilated | solution.py:20
  119.9 5.3 fusion.22
  125.2 3.0 collective-permute-start
  128.2 0.0 copy-start.7
  128.2 0.0 copy-start.6
  128.2 68.4 %collective-permute-done = bf16[3,256,2048]{2,1,0:T(8,128)(2,1)} collective-permute-done((bf16[3,256,2048]{2,1,0:T(8,128)(2,1)}, bf16[3,256,2048]{2,1,0:T(8,128)(2,1)}, u32[]{:S(2)}, u32[]{:S(2)}) %collective-permute-start) | collective-permute-done | bytes 3145760 | tf_op jit(solution)/shard_map/ppermute | solution.py:53
  196.6 10.1 %maximum_select_fusion.2 = bf16[3,256,4096]{2,1,0:T(8,128)(2,1)} fusion(bf16[3,256,2048]{2,1,0:T(8,128)(2,1)} %collective-permute-done, bf16[3,256,2048]{2,1,0:T(8,128)(2,1)} %fusion.22, pred[]{:T(512)S(6)} %eq.41), kind=kLoop, calls=%fused_computation.29 | loop fusion | flops 28311552 | bytes 12582913 | tf_op jit(solution)/shard_map/jit(_where)/select_n | solution.py:56
  206.7 2.8 collective-permute-start.1
  209.5 0.0 copy-done.7
  209.5 0.1 broadcast_bitcast_fusion
  209.6 8.9 %rev.7 = f32[128,2048]{1,0:T(8,128)} reverse(f32[128,2048]{1,0:T(8,128)} %param.17), dimensions={0} | reverse | bytes 2097152 | tf_op jit(solution)/shard_map/rev | solution.py:19
  218.4 0.0 copy-done.6
  218.5 261.0 %collective-permute-done.1 = bf16[3,256,4096]{2,1,0:T(8,128)(2,1)} collective-permute-done((bf16[3,256,4096]{2,1,0:T(8,128)(2,1)}, bf16[3,256,4096]{2,1,0:T(8,128)(2,1)}, u32[]{:S(2)}, u32[]{:S(2)}) %collective-permute-start.1) | collective-permute-done | bytes 6291488 | tf_op jit(solution)/shard_map/ppermute | solution.py:53
  479.4 41.1 %add_convert_fusion = bf16[3,256,2048]{2,1,0:T(8,128)(2,1)} fusion(bf16[8192,2048]{1,0:T(8,128)(2,1)} %param.15, bf16[3,256,4096]{2,1,0:T(8,128)(2,1)} %collective-permute-done.1, bf16[3,256,4096]{2,1,0:T(8,128)(2,1)} %maximum_select_fusion.2, pred[]{:T(512)S(6)} %eq.40, bf16[1,256,2048]{2,1,0:T(8,128)(2,1)S(1)} %bitcast.32, ...), kind=kOutput, calls=%fused_computation.32 | convolution fusion | flops 25832718336 | bytes 52428800 | tf_op jit(solution)/shard_map/rlk,kc->rlc/dot_general | solution.py:59
  520.5 1.3 slice_bitcast_fusion
  521.8 0.0 copy-start.4
  521.8 2.1 fusion.41
  523.9 3.5 fusion.29
  527.4 0.0 copy-done.4
  527.4 0.0 copy-start.3
  527.4 0.0 copy-start.1
  527.4 45.4 %fusion.37 = f32[2,256,2048]{2,0,1:T(2,128)S(1)} fusion(f32[2,256,2048]{2,1,0:T(8,128)S(1)} %fusion.29, f32[128,1,2048]{2,0,1:T(8,128)S(1)} %bitcast.33), kind=kOutput, calls=%fused_computation.54 | convolution fusion | flops 1211105280 | bytes 9437184 | tf_op jit(solution)/shard_map/conv_general_dilated | solution.py:20
  572.9 0.0 copy-done.3
  572.9 4.1 fusion.36
  576.9 0.0 copy-done.1
  (4 shorter events, 0.1 us)
Async XLA Ops:
  0.0 12.9 %copy-start = (bf16[2,32,2048]{2,1,0:T(8,128)(2,1)S(1)}, bf16[2,32,2048]{2,1,0:T(8,128)(2,1)}, u32[]{:S(2)}) copy-start(bf16[2,32,2048]{2,1,0:T(8,128)(2,1)} %param.10) | copy-start | bytes 786436
  0.0 15.4 %copy-start.2 = (bf16[256,2048]{1,0:T(8,128)(2,1)S(1)}, bf16[256,2048]{1,0:T(8,128)(2,1)}, u32[]{:S(2)}) copy-start(bf16[256,2048]{1,0:T(8,128)(2,1)} %param.9) | copy-start | bytes 3145732
  15.8 5.2 copy-start.5
  125.2 71.4 %collective-permute-start = (bf16[3,256,2048]{2,1,0:T(8,128)(2,1)}, bf16[3,256,2048]{2,1,0:T(8,128)(2,1)}, u32[]{:S(2)}, u32[]{:S(2)}) collective-permute-start(bf16[3,256,2048]{2,1,0:T(8,128)(2,1)} %fusion.22), channel_id=1, source_target_pairs={{0,1},{1,0},{2,3},{3,2},{4,5},{5,4},{6,7},{7,6},{8,9},{9,8},{10,11... | collective-permute-start | bytes 9437192 | tf_op jit(solution)/shard_map/ppermute | solution.py:53
  128.2 81.2 %copy-start.7 = (s32[2,2]{1,0:T(2,128)S(1)}, s32[2,2]{1,0:T(2,128)}, u32[]{:S(2)}) copy-start(s32[2,2]{1,0:T(2,128)} %param.12) | copy-start | bytes 52
  128.2 90.2 %copy-start.6 = (f32[7,2048]{1,0:T(8,128)S(1)}, f32[7,2048]{1,0:T(8,128)}, u32[]{:S(2)}) copy-start(f32[7,2048]{1,0:T(8,128)} %param.16) | copy-start | bytes 172036
  206.7 272.7 %collective-permute-start.1 = (bf16[3,256,4096]{2,1,0:T(8,128)(2,1)}, bf16[3,256,4096]{2,1,0:T(8,128)(2,1)}, u32[]{:S(2)}, u32[]{:S(2)}) collective-permute-start(bf16[3,256,4096]{2,1,0:T(8,128)(2,1)} %maximum_select_fusion.2), channel_id=1, source_target_pairs={{0,2},{1,3},{2,0},{3,1},{4,6},{5,7},{6,4},{7,5},{8,10},{9,11},{10,... | collective-permute-start | bytes 18874376 | tf_op jit(solution)/shard_map/ppermute | solution.py:53
  521.8 5.6 copy-start.4
  527.4 45.5 %copy-start.3 = (bf16[3,256,2048]{2,1,0:T(8,128)(2,1)S(1)}, bf16[3,256,2048]{2,1,0:T(8,128)(2,1)}, u32[]{:S(2)}) copy-start(bf16[3,256,2048]{2,1,0:T(8,128)(2,1)} %add_convert_fusion) | copy-start | bytes 9437188
  527.4 49.5 %copy-start.1 = (bf16[2,32,2048]{2,1,0:T(8,128)(2,1)S(1)}, bf16[2,32,2048]{2,1,0:T(8,128)(2,1)}, u32[]{:S(2)}) copy-start(bf16[2,32,2048]{2,1,0:T(8,128)(2,1)} %param.10) | copy-start | bytes 786436
